TPU v7x, 128 devices: a whole 4x4x4 slice. The times are simulated.
128 devices in a mesh: lat: 8 (over x, core), lon: 16 (over y, z).
Axes of the slice: x: 4, y: 4, z: 4, core: 2. Of those that a mesh axis runs over, the one named last changes fastest.
Arguments:
- positions: int32 [9216], P(('lat', 'lon')), may hold values from 0 to 36863, as said below
- encoded: float32 [9216, 1280], P(('lat', 'lon')), may hold values from -6 to 6
- mask_token: float32 [1280], replicated, may hold values from -4 to 4
- norm_gain: float32 [1280], replicated, may hold values from 0.1 to 1.9
- w_query: float32 [1280, 640], replicated
- w_key: float32 [1280, 640], replicated
- w_value: float32 [1280, 640], replicated, may hold values from -0.15625 to 0.15625
- w_out: float32 [640, 1280], replicated, may hold values from -0.25 to 0.25
- cotangent: float32 [96, 384, 1280], P('lat', 'lon'), may hold values from -6 to 6
Outputs:
- decoded: float32 [96, 384, 1280], P('lat', 'lon')
- grad_query: float32 [1280, 640], P('lon')
- grad_key: float32 [1280, 640], P('lon')
- grad_value: float32 [1280, 640], P('lon')
- grad_out: float32 [640, 1280], P('lon')
- grad_mask: float32 [1280], P('lon')
- grad_gain: float32 [1280], P('lon')
- grad_encoded: float32 [9216, 1280], P(('lat', 'lon'))
Inputs may be any that keep to these rules, and one draw needn't show every extreme that they name: All positions are distinct cells, a quarter of the grid. Tile (a, b) is the block of 12 x (24) cells of index a along lat and b along lon. The 72 tokens of one encoder shard hold at most 2 cells of any one tile, and some tile holds exactly 2 from every shard.
All inputs are finite; a program needn't handle non-finite values.
Results may differ from a plain program's by a relative error of at most 0.0003.
Values sent between devices are 32-bit elements; how exact they have to be, the bound alone decides.
A program may use at most 192 MiB of HBM per device.

v0:
```python
import math

import jax
import jax.numpy as jnp
from jax import lax
from jax.sharding import PartitionSpec as P

HEAD = 80


highest = lax.Precision.HIGHEST


def passed_along(block, axis, distance):
    devices = range(lax.axis_size(axis))
    route = [((i - distance) % len(devices), i) for i in devices]
    return lax.ppermute(block, axis, route)


def window_block(tile_grid, gain_vec, query_w, key_w, value_w, out_w, is_last):
    tile_rows, tile_cols, model_width = tile_grid.shape
    window_count = tile_cols // tile_rows
    window_area = tile_rows * tile_rows
    tokens = tile_grid.reshape(tile_rows, window_count, tile_rows, model_width).transpose(
        1, 0, 2, 3
    )
    tokens = tokens.reshape(window_count, window_area, model_width)
    centred = tokens - jnp.mean(tokens, axis=-1, keepdims=True)
    variance = jnp.mean(centred * centred, axis=-1, keepdims=True)
    normed = centred * lax.rsqrt(variance + 1e-05) * gain_vec
    flat_rows = normed.reshape(window_count * window_area, model_width)
    inner_width = query_w.shape[1]
    head_count = inner_width // HEAD
    query = jnp.dot(flat_rows, query_w, precision=highest).reshape(
        window_count, window_area, head_count, HEAD
    )
    key_rows = jnp.dot(flat_rows, key_w, precision=highest).reshape(
        window_count, window_area, head_count, HEAD
    )
    values = jnp.dot(flat_rows, value_w, precision=highest).reshape(
        window_count, window_area, head_count, HEAD
    )
    scores = jnp.einsum("wqhe,wkhe->whqk", query, key_rows, precision=highest) / math.sqrt(HEAD)
    window_row = jnp.arange(window_area) // tile_rows
    wrapped = jnp.logical_and(window_row >= tile_rows - tile_rows // 2, is_last)
    allowed = wrapped[:, None] == wrapped[None, :]
    scores = jnp.where(allowed, scores, -1e30)
    row_max = lax.stop_gradient(jnp.max(scores, axis=-1, keepdims=True))
    exponent = jnp.exp(scores - row_max)
    weights = exponent / jnp.sum(exponent, axis=-1, keepdims=True)
    attended = jnp.einsum("whqk,wkhe->wqhe", weights, values, precision=highest)
    attended = attended.reshape(window_count * window_area, inner_width)
    update = jnp.dot(attended, out_w, precision=highest).reshape(
        window_count, window_area, model_width
    )
    result = tokens + update
    result = result.reshape(window_count, tile_rows, tile_rows, model_width).transpose(1, 0, 2, 3)
    return result.reshape(tile_rows, tile_cols, model_width)


def move_tile(tile_grid, direction):
    margin = tile_grid.shape[0] // 2
    if direction < 0:
        edge_cols = tile_grid[:, :margin]
    else:
        edge_cols = tile_grid[:, -margin:]
    arrived = passed_along(edge_cols, "lon", direction)
    if direction < 0:
        tile_grid = jnp.concatenate([tile_grid[:, margin:], arrived], axis=1)
        edge_rows = tile_grid[:margin]
    else:
        tile_grid = jnp.concatenate([arrived, tile_grid[:, :-margin]], axis=1)
        edge_rows = tile_grid[-margin:]
    arrived = passed_along(edge_rows, "lat", direction)
    if direction < 0:
        return jnp.concatenate([tile_grid[margin:], arrived], axis=0)
    return jnp.concatenate([arrived, tile_grid[:-margin]], axis=0)


def own_rows(whole, lon_count):
    share = whole.shape[0] // lon_count
    return lax.dynamic_slice_in_dim(whole, lax.axis_index("lon") * share, share, 0)


def body(positions, encoded, mask_token, norm_gain, w_query, w_key, w_value, w_out, cotangent):
    tile_rows, tile_cols, model_width = cotangent.shape
    lat_count = lax.axis_size("lat")
    lon_count = lax.axis_size("lon")
    devices = lat_count * lon_count
    grid_lat = lat_count * tile_rows
    grid_lon = lon_count * tile_cols
    tile_size = tile_rows * tile_cols
    capacity = tile_size // devices
    lat_cell = positions // grid_lon
    lon_cell = positions % grid_lon
    target = lat_cell // tile_rows * lon_count + lon_cell // tile_cols
    cell_slot = lat_cell % tile_rows * tile_cols + lon_cell % tile_cols
    serial = jnp.arange(positions.shape[0])
    earlier = jnp.logical_and(target[None, :] == target[:, None], serial[None, :] < serial[:, None])
    rank = jnp.sum(earlier.astype(jnp.int32), axis=1)
    buffer_index = target * capacity + rank
    send_feat = (
        jnp.zeros((devices * capacity, model_width), jnp.float32).at[buffer_index].set(encoded)
    )
    send_slot = (
        jnp.full((devices * capacity,), tile_size, jnp.int32).at[buffer_index].set(cell_slot)
    )
    recv_feat, recv_slot = (
        lax.all_to_all(
            send_feat.reshape(devices, capacity, model_width),
            ("lat", "lon"),
            split_axis=0,
            concat_axis=0,
            tiled=True,
        ),
        lax.all_to_all(
            send_slot.reshape(devices, capacity),
            ("lat", "lon"),
            split_axis=0,
            concat_axis=0,
            tiled=True,
        ),
    )
    recv_feat = recv_feat.reshape(devices * capacity, model_width)
    recv_slot = recv_slot.reshape(devices * capacity)
    filled = (
        jnp.broadcast_to(mask_token, (tile_size, model_width))
        .at[recv_slot]
        .set(recv_feat, mode="drop")
    )
    visible = jnp.zeros((tile_size,), jnp.float32).at[recv_slot].set(1.0, mode="drop")
    filled = filled.reshape(tile_rows, tile_cols, model_width)
    rolled = move_tile(filled, -1)
    is_last = lax.axis_index("lat") == lat_count - 1

    def forward(tile_grid, gain_vec, query_w, key_w, value_w, out_w):
        return window_block(tile_grid, gain_vec, query_w, key_w, value_w, out_w, is_last)

    out_rolled, pullback = jax.vjp(forward, rolled, norm_gain, w_query, w_key, w_value, w_out)
    decoded = move_tile(out_rolled, 1)
    grad_rolled = move_tile(cotangent, -1)
    grad_tile, grad_gain, grad_query, grad_key, grad_value, grad_out = pullback(grad_rolled)
    grad_cells = move_tile(grad_tile, 1).reshape(tile_size, model_width)
    grad_mask = jnp.sum((1.0 - visible)[:, None] * grad_cells, axis=0)
    valid = recv_slot < tile_size
    send_back = jnp.where(valid[:, None], grad_cells[jnp.minimum(recv_slot, tile_size - 1)], 0.0)
    returned = lax.all_to_all(
        send_back.reshape(devices, capacity, model_width),
        ("lat", "lon"),
        split_axis=0,
        concat_axis=0,
        tiled=True,
    )
    grad_encoded = returned.reshape(devices * capacity, model_width)[buffer_index]
    scale = 1.0 / math.sqrt(grid_lat * grid_lon)
    totals = lax.psum(
        (
            grad_query * scale,
            grad_key * scale,
            grad_value * scale,
            grad_out * scale,
            grad_mask * scale,
            grad_gain * scale,
        ),
        ("lat", "lon"),
    )
    summed = tuple((own_rows(total, lon_count) for total in totals))
    return (decoded, summed[0], summed[1], summed[2], summed[3], summed[4], summed[5], grad_encoded)


def solution(mesh):
    return jax.shard_map(
        body,
        mesh=mesh,
        in_specs=(
            P(("lat", "lon")),
            P(("lat", "lon"), None),
            P(),
            P(),
            P(),
            P(),
            P(),
            P(),
            P("lat", "lon", None),
        ),
        out_specs=(
            P("lat", "lon", None),
            P("lon", None),
            P("lon", None),
            P("lon", None),
            P("lon", None),
            P("lon"),
            P("lon"),
            P(("lat", "lon"), None),
        ),
        check_vma=False,
    )
```

profile of v0, /device:TPU:0, one launch (start us, length us, event | category | flops | bytes accessed | tf_op | source)
XLA Modules:
  0.0 437.2 jit_solution(4705663735451628186)
XLA Ops:
  10.6 11.1 %all-to-all-start = ((s32[128,1,2]{2,1,0:T(1,128)}), s32[128,1,2]{2,1,0:T(1,128)S(1)}, u32[]{:S(2)}, u32[]{:S(2)}) async-start(s32[128,1,2]{2,1,0:T(1,128)} %bitcast), calls=%async_computation | async-start | bytes 131072 | tf_op jit(solution)/shard_map/all_to_all | solution.py:116
  24.2 3.0 reshape.402
  27.1 4.1 all-to-all-done
  31.2 6.2 %all-to-all-start.1 = ((f32[128,2,1280]{2,1,0:T(2,128)}), f32[128,2,1280]{2,1,0:T(2,128)}, u32[]{:S(2)}, u32[]{:S(2)}) async-start(f32[128,2,1280]{2,1,0:T(2,128)} %reshape.402), calls=%async_computation.1 | async-start | bytes 2621440 | tf_op jit(solution)/shard_map/all_to_all | solution.py:109
  39.3 5.1 %collective-permute-start.4 = (f32[12,6,1280]{2,1,0:T(8,128)}, f32[12,6,1280]{2,1,0:T(8,128)}, u32[]{:S(2)}, u32[]{:S(2)}) collective-permute-start(f32[12,6,1280]{2,1,0:T(8,128)} %slice.57), channel_id=1, source_target_pairs={{1,0},{2,1},{3,2},{4,3},{5,4},{6,5},{7,6},{8,7},{9,8},{10,9},{11,1... | collective-permute-start | bytes 1105928 | tf_op jit(solution)/shard_map/ppermute | solution.py:17
  44.3 2.6 slice.56
  48.4 10.4 %all-to-all-done.1 = f32[128,2,1280]{2,1,0:T(2,128)} async-done(((f32[128,2,1280]{2,1,0:T(2,128)}), f32[128,2,1280]{2,1,0:T(2,128)}, u32[]{:S(2)}, u32[]{:S(2)}) %all-to-all-start.1) | async-done | bytes 1310752 | tf_op jit(solution)/shard_map/all_to_all | solution.py:109
  58.8 3.0 reshape.456
  63.0 4.7 %scatter_fusion = f32[288,1280]{1,0:T(8,128)} fusion(f32[288,1280]{1,0:T(8,128)} %broadcast_in_dim.71, s32[256]{0:T(256)S(1)} %bitcast.126, f32[256,1280]{1,0:T(8,128)} %reshape.456), kind=kCustom, calls=%fused_computation.4 | custom fusion | bytes 3933184 | tf_op jit(solution)/shard_map/scatter | solution.py:129
  69.6 3.0 collective-permute-start
  72.6 2.7 fusion.24
  76.8 6.1 %collective-permute-done = f32[12,6,1280]{2,1,0:T(8,128)} collective-permute-done((f32[12,6,1280]{2,1,0:T(8,128)}, f32[12,6,1280]{2,1,0:T(8,128)}, u32[]{:S(2)}, u32[]{:S(2)}) %collective-permute-start) | collective-permute-done | bytes 368672 | tf_op jit(solution)/shard_map/ppermute | solution.py:17
  85.3 4.5 %copy.148 = f32[1280,640]{0,1:T(8,128)} copy(f32[1280,640]{1,0:T(8,128)} %param.13) | data formatting | bytes 6553600 | tf_op args[4]
  89.9 4.6 %copy.150 = f32[1280,640]{0,1:T(8,128)} copy(f32[1280,640]{1,0:T(8,128)} %param.14) | data formatting | bytes 6553600 | tf_op args[5]
  94.5 4.6 %copy.146 = f32[1280,640]{0,1:T(8,128)} copy(f32[1280,640]{1,0:T(8,128)} %param.15) | data formatting | bytes 6553600 | tf_op args[6]
  99.1 2.5 pad_maximum_fusion.3
  101.6 2.6 reshape.409
  104.2 3.9 copy.158
  109.6 2.6 reshape.414
  112.1 7.4 %fusion.14 = f32[2,8,80,144]{2,3,1,0:T(8,128)} fusion(f32[8,80,1280,1]{2,1,0,3:T(8,128)S(1)} %bitcast.105, f32[2,144,1280,1]{2,0,1,3:T(2,128)} %bitcast.123), kind=kOutput, calls=%fused_computation.52 | convolution fusion | flops 2831155200 | bytes 5488640 | tf_op jit(solution)/shard_map/transpose(jvp())/dot_general | solution.py:53
  121.9 2.7 reshape.405
  131.3 5.0 %fusion.19 = f32[2,144,8,80]{3,1,2,0:T(8,128)S(1)} fusion(f32[8,80,1280,1]{2,1,0,3:T(8,128)S(1)} %bitcast.115, f32[2,144,1280,1]{2,0,1,3:T(2,128)S(1)} %bitcast.116), kind=kOutput, calls=%fused_computation.56 | convolution fusion | flops 2831155200 | bytes 5488640 | tf_op jit(solution)/shard_map/jvp()/dot_general | solution.py:34
  136.2 5.2 %fusion.17 = f32[2,144,8,80]{3,1,2,0:T(8,128)S(1)} fusion(f32[8,80,1280,1]{2,1,0,3:T(8,128)S(1)} %bitcast.114, f32[2,144,1280,1]{2,0,1,3:T(2,128)S(1)} %bitcast.117), kind=kOutput, calls=%fused_computation.54 | convolution fusion | flops 2831155200 | bytes 5488640 | tf_op jit(solution)/shard_map/jvp()/dot_general | solution.py:37
  145.1 3.7 convolution_bitcast_fusion
  148.9 5.0 %fusion.21 = f32[2,144,8,80]{3,1,2,0:T(8,128)S(1)} fusion(f32[8,80,1280,1]{2,1,0,3:T(8,128)S(1)} %bitcast.113, f32[2,144,1280,1]{2,0,1,3:T(2,128)S(1)} %bitcast.118), kind=kOutput, calls=%fused_computation.58 | convolution fusion | flops 2831155200 | bytes 5488640 | tf_op jit(solution)/shard_map/jvp()/dot_general | solution.py:40
  153.9 6.8 %convolution_bitcast_fusion.3 = f32[2,144,8,80]{3,1,2,0:T(8,128)} fusion(f32[2,144,8,80]{3,1,2,0:T(8,128)S(1)} %fusion.21, f32[2,8,144]{2,1,0:T(8,128)S(1)} %fusion.30, f32[2,8,144,144]{2,3,1,0:T(8,128)S(1)} %get-tuple-element.31, f32[2,8,144]{2,1,0:T(8,128)S(1)} %get-tuple-element.30, pred[144,144]{0,1:T(8,128)(4,1)S(1)} %broadcast_compare_fusion), kind=kOutput, calls=%fused_computation.51 | convolution fusion | flops 319832064 | bytes 2840832 | tf_op jit(solution)/shard_map/jvp(whqk,wkhe->wqhe)/dot_general | solution.py:51
  160.7 2.8 multiply_reduce_fusion
  163.5 4.1 convolution_bitcast_fusion.1
  167.6 7.0 %convolution_bitcast_fusion.2 = f32[2,144,8,80]{3,1,2,0:T(8,128)} fusion(f32[2,144,8,80]{3,1,2,0:T(8,128)S(1)} %fusion.17, f32[2,8,144,144]{2,3,1,0:T(8,128)S(1)} %get-tuple-element.33, f32[2,8,144]{2,1,0:T(8,128)S(1)} %neg.9, f32[2,8,144]{2,1,0:T(8,128)S(1)} %fusion.30, pred[144,144]{0,1:T(8,128)(4,1)S(1)} %broadcast_compare_fusion, ...), kind=kOutput, calls=%fused_computation.50 | convolution fusion | flops 321159168 | bytes 4177152 | tf_op jit(solution)/shard_map/transpose(jvp(wqhe,wkhe->whqk))/dot_general | solution.py:43
  174.6 2.5 mul.216
  177.2 3.0 copy.168
  180.2 2.6 reshape.416
  182.8 2.7 copy.163
  188.0 2.7 copy.153
  192.1 2.5 reshape.410
  194.6 2.7 copy.162
  197.3 2.5 reshape.411
  199.8 2.5 reshape.413
  202.3 9.0 %convolution_multiply_fusion.1 = f32[1280,640]{1,0:T(8,128)} fusion(f32[288,1280]{1,0:T(8,128)} %mul.216, f32[288,640]{1,0:T(8,128)} %reshape.412), kind=kOutput, calls=%fused_computation.7 | convolution fusion | flops 2831974400 | bytes 5488640 | tf_op jit(solution)/shard_map/transpose(jvp())/dot_general | solution.py:40
  211.4 7.7 %convolution_multiply_fusion.3 = f32[1280,640]{1,0:T(8,128)} fusion(f32[288,1280]{1,0:T(8,128)S(1)} %copy-done.6, f32[288,640]{1,0:T(8,128)S(1)} %copy-done.10), kind=kOutput, calls=%fused_computation.9 | convolution fusion | flops 2831974400 | bytes 5488640 | tf_op jit(solution)/shard_map/transpose(jvp())/dot_general | solution.py:34
  219.1 8.1 %convolution_multiply_fusion.2 = f32[1280,640]{1,0:T(8,128)} fusion(f32[288,1280]{1,0:T(8,128)S(1)} %copy-done.6, f32[288,640]{1,0:T(8,128)S(1)} %copy-done.12), kind=kOutput, calls=%fused_computation.8 | convolution fusion | flops 2831974400 | bytes 5488640 | tf_op jit(solution)/shard_map/transpose(jvp())/dot_general | solution.py:37
  227.2 7.2 %convolution_multiply_fusion = f32[640,1280]{1,0:T(8,128)} fusion(f32[288,640]{1,0:T(8,128)S(1)} %copy-done.16, f32[288,1280]{1,0:T(8,128)S(1)} %copy-done.14), kind=kOutput, calls=%fused_computation.6 | convolution fusion | flops 2831974400 | bytes 5488640 | tf_op jit(solution)/shard_map/transpose(jvp())/dot_general | solution.py:53
  234.5 6.1 %fusion.44 = f32[288,1280]{1,0:T(8,128)S(1)} fusion(f32[288,640]{1,0:T(8,128)} %reshape.412, f32[1280,640]{1,0:T(8,128)} %param.15), kind=kOutput, calls=%fused_computation.117 | convolution fusion | flops 2831155200 | bytes 5488640 | tf_op jit(solution)/shard_map/transpose(jvp())/dot_general | solution.py:40
  240.6 4.0 convolution_add_fusion.1
  244.6 5.0 %convolution_add_fusion = f32[288,1280]{1,0:T(8,128)} fusion(f32[288,1280]{1,0:T(8,128)S(1)} %convolution_add_fusion.1, f32[288,640]{1,0:T(8,128)S(1)} %copy-done.11, f32[1280,640]{1,0:T(8,128)S(1)} %copy-done.8), kind=kOutput, calls=%fused_computation.14 | convolution fusion | flops 2831523840 | bytes 6963200 | tf_op jit(solution)/shard_map/transpose(jvp())/dot_general | solution.py:34
  249.6 2.7 reshape.415
  252.3 2.8 multiply_reduce_fusion.1
  255.3 2.5 multiply_reduce_fusion.3
  258.0 4.9 %fusion.8 = f32[12,2,12,1280]{3,2,1,0:T(8,128)} fusion(f32[2,12,12,1280]{3,2,1,0:T(8,128)} %reshape.415, f32[2,12,12]{2,0,1:T(2,128)S(1)} %copy.171, f32[2,12,12]{2,0,1:T(2,128)S(1)} %get-tuple-element.24, f32[1280]{0:T(1024)S(1)} %copy-done.18, f32[2,12,12]{2,0,1:T(2,128)S(1)} %fusion.42, f32[2,12,12]{2,0,1:T(2,128)S(1)} %broadcast_multiply_fusion, ...), kind=kLoop, calls=%fused_computation.24 | loop fusion | flops 2949120 | bytes 5907968 | tf_op jit(solution)/shard_map/transpose(jvp())/transpose | solution.py:24
  262.9 2.6 reshape.417
  269.4 18.8 %collective-permute-done.6 = f32[12,6,1280]{2,1,0:T(8,128)} collective-permute-done((f32[12,6,1280]{2,1,0:T(8,128)}, f32[12,6,1280]{2,1,0:T(8,128)}, u32[]{:S(2)}, u32[]{:S(2)}) %collective-permute-start.6) | collective-permute-done | bytes 368672 | tf_op jit(solution)/shard_map/ppermute | solution.py:17
  290.8 3.8 copy.144
  294.6 2.5 dot_general.83
  297.1 5.4 %fusion.2 = f32[2,144,1280]{2,1,0:T(8,128)S(1)} fusion(f32[2,144,640]{2,1,0:T(8,128)} %dot_general.83, f32[640,1280]{1,0:T(8,128)S(1)} %copy-done, f32[2,144,1280]{2,0,1:T(2,128)} %bitcast.124), kind=kOutput, calls=%fused_computation.13 | convolution fusion | flops 2831523840 | bytes 6963200 | tf_op jit(solution)/shard_map/jvp()/dot_general | solution.py:53
  305.1 2.6 reshape.408
  309.5 2.7 multiply_reduce_fusion.4
  312.3 4.2 gather_fusion
  316.5 2.9 gather.9
  319.4 3.0 broadcast_select_fusion
  322.4 9.9 %all-to-all-start.2 = ((f32[128,2,1280]{2,1,0:T(2,128)}), f32[128,2,1280]{2,1,0:T(2,128)}, u32[]{:S(2)}, u32[]{:S(2)}) async-start(f32[128,2,1280]{2,1,0:T(2,128)} %broadcast_select_fusion), calls=%async_computation.2 | async-start | bytes 2621440 | tf_op jit(solution)/shard_map/all_to_all | solution.py:147
  334.6 80.6 %all-reduce = (f32[1280]{0:T(1024)S(1)}, f32[1280]{0:T(1024)S(1)}) all-reduce(f32[1280]{0:T(1024)S(1)} %get-tuple-element.37, f32[1280]{0:T(1024)S(1)} %get-tuple-element.36), channel_id=1, replica_groups=mesh['lat'=8,'lon'=16] {'lat','lon'}, use_global_device_ids=true, to_apply=%region_17.18 | all-reduce | flops 2560 | bytes 20480 | tf_op jit(solution)/shard_map/psum | solution.py:156
  416.3 2.7 fusion.11
  419.1 3.0 reshape.419
  422.1 2.9 gather_fusion.1
  (121 shorter events, 53.7 us)
Async XLA Ops:
  7.2 105.0 %copy-start = (f32[640,1280]{1,0:T(8,128)S(1)}, f32[640,1280]{1,0:T(8,128)}, u32[]{:S(2)}) copy-start(f32[640,1280]{1,0:T(8,128)} %param.16) | copy-start | bytes 9830404
  10.6 20.6 %all-to-all-start = ((s32[128,1,2]{2,1,0:T(1,128)}), s32[128,1,2]{2,1,0:T(1,128)S(1)}, u32[]{:S(2)}, u32[]{:S(2)}) async-start(s32[128,1,2]{2,1,0:T(1,128)} %bitcast), calls=%async_computation | async-start | bytes 131072 | tf_op jit(solution)/shard_map/all_to_all | solution.py:116
  31.2 27.6 %all-to-all-start.1 = ((f32[128,2,1280]{2,1,0:T(2,128)}), f32[128,2,1280]{2,1,0:T(2,128)}, u32[]{:S(2)}, u32[]{:S(2)}) async-start(f32[128,2,1280]{2,1,0:T(2,128)} %reshape.402), calls=%async_computation.1 | async-start | bytes 2621440 | tf_op jit(solution)/shard_map/all_to_all | solution.py:109
  37.4 387.7 %all-reduce.4.cloned.1.call-start = ((), (), s32[]{:S(2)}) async-start(), calls=%async_computation.3 | async-start | bytes 26214400 | tf_op jit(solution)/shard_map/psum | solution.py:156
  39.3 33.3 %collective-permute-start.4 = (f32[12,6,1280]{2,1,0:T(8,128)}, f32[12,6,1280]{2,1,0:T(8,128)}, u32[]{:S(2)}, u32[]{:S(2)}) collective-permute-start(f32[12,6,1280]{2,1,0:T(8,128)} %slice.57), channel_id=1, source_target_pairs={{1,0},{2,1},{3,2},{4,3},{5,4},{6,5},{7,6},{8,7},{9,8},{10,9},{11,1... | collective-permute-start | bytes 1105928 | tf_op jit(solution)/shard_map/ppermute | solution.py:17
  46.9 14.9 %copy-start.19 = (f32[1280]{0:T(1024)S(1)}, f32[1280]{0:T(1024)}, u32[]{:S(2)}) copy-start(f32[1280]{0:T(1024)} %param.11) | copy-start | bytes 15364
  69.6 13.3 %collective-permute-start = (f32[12,6,1280]{2,1,0:T(8,128)}, f32[12,6,1280]{2,1,0:T(8,128)}, u32[]{:S(2)}, u32[]{:S(2)}) collective-permute-start(f32[12,6,1280]{2,1,0:T(8,128)} %slice.69), channel_id=1, source_target_pairs={{1,0},{2,1},{3,2},{4,3},{5,4},{6,5},{7,6},{8,7},{9,8},{10,9},{11,1... | collective-permute-start | bytes 1105928 | tf_op jit(solution)/shard_map/ppermute | solution.py:17
  75.3 23.8 %collective-permute-start.5 = (f32[6,24,1280]{2,1,0:T(8,128)}, f32[6,24,1280]{2,1,0:T(8,128)}, u32[]{:S(2)}, u32[]{:S(2)}) collective-permute-start(f32[6,24,1280]{2,1,0:T(8,128)} %get-tuple-element.21), channel_id=1, source_target_pairs={{16,0},{32,16},{48,32},{64,48},{80,64},{96,80},{112,96},{0,112},{1... | collective-permute-start | bytes 2211848 | tf_op jit(solution)/shard_map/ppermute | solution.py:17
  85.2 34.3 %collective-permute-start.1 = (f32[6,24,1280]{2,1,0:T(8,128)}, f32[6,24,1280]{2,1,0:T(8,128)}, u32[]{:S(2)}, u32[]{:S(2)}) collective-permute-start(f32[6,24,1280]{2,1,0:T(8,128)} %get-tuple-element.23), channel_id=1, source_target_pairs={{16,0},{32,16},{48,32},{64,48},{80,64},{96,80},{112,96},{0,112},{1... | collective-permute-start | bytes 2211848 | tf_op jit(solution)/shard_map/ppermute | solution.py:17
  104.2 3.9 copy-start.2
  112.1 7.4 %copy-start.15 = (f32[6,24,1280]{2,1,0:T(8,128)S(1)}, f32[6,24,1280]{2,1,0:T(8,128)}, u32[]{:S(2)}) copy-start(f32[6,24,1280]{2,1,0:T(8,128)} %get-tuple-element.22) | copy-start | bytes 2211844
  124.6 2.1 copy-start.1
  124.6 2.5 copy-start.18
  128.6 2.6 copy-start.5
  131.3 5.0 %copy-start.4 = (f32[1280,640]{0,1:T(8,128)S(1)}, f32[1280,640]{0,1:T(8,128)}, u32[]{:S(2)}) copy-start(f32[1280,640]{0,1:T(8,128)} %copy.150) | copy-start | bytes 9830404
  143.9 1.3 copy-start.9
  145.1 3.7 copy-start.3
  188.0 2.7 copy-start.17
  202.3 9.0 %copy-start.6 = (f32[288,1280]{1,0:T(8,128)S(1)}, f32[288,1280]{1,0:T(8,128)}, u32[]{:S(2)}) copy-start(f32[288,1280]{1,0:T(8,128)} %mul.216) | copy-start | bytes 4423684
  202.3 9.0 %copy-start.10 = (f32[288,640]{1,0:T(8,128)S(1)}, f32[288,640]{1,0:T(8,128)}, u32[]{:S(2)}) copy-start(f32[288,640]{1,0:T(8,128)} %reshape.410) | copy-start | bytes 2211844
  211.4 7.7 %copy-start.12 = (f32[288,640]{1,0:T(8,128)S(1)}, f32[288,640]{1,0:T(8,128)}, u32[]{:S(2)}) copy-start(f32[288,640]{1,0:T(8,128)} %reshape.411) | copy-start | bytes 2211844
  219.1 8.1 %copy-start.14 = (f32[288,1280]{1,0:T(8,128)S(1)}, f32[288,1280]{1,0:T(8,128)}, u32[]{:S(2)}) copy-start(f32[288,1280]{1,0:T(8,128)} %reshape.414) | copy-start | bytes 4423684
  219.1 8.1 %copy-start.16 = (f32[288,640]{1,0:T(8,128)S(1)}, f32[288,640]{1,0:T(8,128)}, u32[]{:S(2)}) copy-start(f32[288,640]{1,0:T(8,128)} %reshape.413) | copy-start | bytes 2211844
  234.4 6.1 %copy-start.7 = (f32[1280,640]{1,0:T(8,128)S(1)}, f32[1280,640]{1,0:T(8,128)}, u32[]{:S(2)}) copy-start(f32[1280,640]{1,0:T(8,128)} %param.14) | copy-start | bytes 9830404
  234.4 6.1 %copy-start.13 = (f32[288,640]{1,0:T(8,128)S(1)}, f32[288,640]{1,0:T(8,128)}, u32[]{:S(2)}) copy-start(f32[288,640]{1,0:T(8,128)} %reshape.411) | copy-start | bytes 2211844
  240.5 4.1 copy-start.8
  240.6 4.1 copy-start.11
  267.4 20.8 %collective-permute-start.6 = (f32[12,6,1280]{2,1,0:T(8,128)}, f32[12,6,1280]{2,1,0:T(8,128)}, u32[]{:S(2)}, u32[]{:S(2)}) collective-permute-start(f32[12,6,1280]{2,1,0:T(8,128)} %slice.78), channel_id=1, source_target_pairs={{15,0},{0,1},{1,2},{2,3},{3,4},{4,5},{5,6},{6,7},{7,8},{8,9},{9,10... | collective-permute-start | bytes 1105928 | tf_op jit(solution)/shard_map/ppermute | solution.py:17
  290.4 19.1 %collective-permute-start.7 = (f32[6,24,1280]{2,1,0:T(8,128)}, f32[6,24,1280]{2,1,0:T(8,128)}, u32[]{:S(2)}, u32[]{:S(2)}) collective-permute-start(f32[6,24,1280]{2,1,0:T(8,128)} %fusion.23), channel_id=1, source_target_pairs={{112,0},{0,16},{16,32},{32,48},{48,64},{64,80},{80,96},{96,112},{1... | collective-permute-start | bytes 2211848 | tf_op jit(solution)/shard_map/ppermute | solution.py:17
  309.5 22.8 %collective-permute-start.2 = (f32[12,6,1280]{2,1,0:T(8,128)}, f32[12,6,1280]{2,1,0:T(8,128)}, u32[]{:S(2)}, u32[]{:S(2)}) collective-permute-start(f32[12,6,1280]{2,1,0:T(8,128)} %slice.72), channel_id=1, source_target_pairs={{15,0},{0,1},{1,2},{2,3},{3,4},{4,5},{5,6},{6,7},{7,8},{8,9},{9,10... | collective-permute-start | bytes 1105928 | tf_op jit(solution)/shard_map/ppermute | solution.py:17
  322.4 96.7 %all-to-all-start.2 = ((f32[128,2,1280]{2,1,0:T(2,128)}), f32[128,2,1280]{2,1,0:T(2,128)}, u32[]{:S(2)}, u32[]{:S(2)}) async-start(f32[128,2,1280]{2,1,0:T(2,128)} %broadcast_select_fusion), calls=%async_computation.2 | async-start | bytes 2621440 | tf_op jit(solution)/shard_map/all_to_all | solution.py:147
  334.5 81.8 %collective-permute-start.3 = (f32[6,24,1280]{2,1,0:T(8,128)}, f32[6,24,1280]{2,1,0:T(8,128)}, u32[]{:S(2)}, u32[]{:S(2)}) collective-permute-start(f32[6,24,1280]{2,1,0:T(8,128)} %fusion.25), channel_id=1, source_target_pairs={{112,0},{0,16},{16,32},{32,48},{48,64},{64,80},{80,96},{96,112},{1... | collective-permute-start | bytes 2211848 | tf_op jit(solution)/shard_map/ppermute | solution.py:17
Sparse Core Ops, SparseCore 0:
  234.6 185.9 all-reduce.3
where the time goes:
time: 445 us; the launch traced here: 437 us
  local copies, waits for them, and re-layouts  126 us (28%)
  matrix products  102 us (23%)
  blocking collectives  80.6 us (18%)
  waiting for transfers between devices  39.4 us (9%)
  other arithmetic  39 us (9%)
  starting transfers between devices  35.7 us (8%)
  between operations  14.8 us (3%)
    psum x1, blocking collectives, body(): lax.psum((grad_query * scale, grad_key * scale, grad_value * scale, grad_...  80.6 us
    ppermute x8, waiting for transfers between devices, passed_along(): return lax.ppermute(block, axis, route)  25 us
    dot_general x3, matrix products, window_block(): jnp.dot(attended, out_w, precision=highest)  20.1 us
    dot_general x3, matrix products, window_block(): jnp.dot(flat_rows, value_w, precision=highest)  20.1 us
    dot_general x3, matrix products, window_block(): jnp.dot(flat_rows, query_w, precision=highest)  17.6 us
    dot_general x3, matrix products, window_block(): jnp.dot(flat_rows, key_w, precision=highest)  17.4 us
    unnamed x43, local copies, waits for them, and re-layouts  16 us
    dot_general x3, matrix products, window_block(): jnp.einsum('wqhe,wkhe->whqk', query, key_rows, precision=highest)  13.4 us
  transfers between devices with their start and end apart: 12, of which 4 were waited for; matrix products, arithmetic and copies ran while one was open for 33% of the time, Pallas kernels for 0%

commit v1 on v0

v1 whole, which is shorter than its diff:
```python
import functools, math
import jax, jax.numpy as jnp
import numpy as np
from jax import lax
from jax.experimental import pallas as pl
from jax.experimental.pallas import tpu as pltpu
from jax.sharding import PartitionSpec as P

HEAD = 80
F32 = jnp.float32
BF16 = jnp.bfloat16


def split(x):
    hi = x.astype(BF16)
    return hi, (x - hi.astype(F32)).astype(BF16)


NN = (((1,), (0,)), ((), ()))
NT = (((1,), (1,)), ((), ()))
TN = (((0,), (0,)), ((), ()))


def dot(a, b, dims):
    return lax.dot_general(a, b, dims, preferred_element_type=F32)


def dot3(a, b, dims):
    return dot(a[0], b[0], dims) + (dot(a[0], b[1], dims) + dot(a[1], b[0], dims))


def head_lanes(h):
    low = h * HEAD // 128 * 128
    high = -(-(h + 1) * HEAD // 128) * 128
    return low, high


def compute_kernel(
    flag_ref, t_ref, g_ref, gain_ref, wq_hbm, wk_hbm, wv_hbm, wo_hbm,
    out_ref, dt_ref, dgain_ref, n_hi, n_lo, g_hi, g_lo, a_hi, a_lo, d_hi, d_lo,
    stage_a, stage_b, wqkv_hi, wqkv_lo, wo_hi, wo_lo,
    xhat_ref, rstd_ref, qkv_ref, att_ref, datt_ref, dqkv_ref, sems,
):
    rows, width = t_ref.shape
    inner = wo_hbm.shape[0]
    heads = inner // HEAD
    half = rows // 2

    load_o = pltpu.make_async_copy(wo_hbm, stage_b, sems.at[0])
    load_q = pltpu.make_async_copy(wq_hbm, stage_a.at[0], sems.at[1])
    load_k = pltpu.make_async_copy(wk_hbm, stage_a.at[1], sems.at[2])
    load_o.start()
    load_q.start()
    load_k.start()

    step = 32
    @pl.loop(0, rows // step)
    def _(i):
        r = pl.ds(pl.multiple_of(i * step, step), step)
        t = t_ref[r, :]
        c = t - jnp.mean(t, axis=-1, keepdims=True)
        rstd = lax.rsqrt(jnp.mean(c * c, axis=-1, keepdims=True) + 1e-5)
        xhat = c * rstd
        xhat_ref[r, :] = xhat
        rstd_ref[r, :] = rstd
        n_hi[r, :], n_lo[r, :] = split(xhat * gain_ref[...])
        g_hi[r, :], g_lo[r, :] = split(g_ref[r, :])

    load_o.wait()

    @pl.loop(0, inner // 32)
    def _(i):
        r = pl.ds(pl.multiple_of(i * 32, 32), 32)
        wo_hi[r, :], wo_lo[r, :] = split(stage_b[r, :])

    @pl.loop(0, inner // 128)
    def _(j):
        c = pl.ds(pl.multiple_of(j * 128, 128), 128)
        datt_ref[:, c] = dot3((g_hi[...], g_lo[...]), (wo_hi[c, :], wo_lo[c, :]), NT)

    def project(which, load, slot):
        load.wait()

        @pl.loop(0, width // 64)
        def _(i):
            r = pl.ds(pl.multiple_of(i * 64, 64), 64)
            c = slice(which * inner, (which + 1) * inner)
            wqkv_hi[r, c], wqkv_lo[r, c] = split(stage_a[slot, r, :])

    project(0, load_q, 0)
    load_v = pltpu.make_async_copy(wv_hbm, stage_a.at[0], sems.at[1])
    load_v.start()
    project(1, load_k, 1)
    project(2, load_v, 0)

    wide = 3 * inner
    full = wide // 256

    @pl.loop(0, full)
    def _(j):
        c = pl.ds(pl.multiple_of(j * 256, 256), 256)
        qkv_ref[:, c] = dot3((n_hi[...], n_lo[...]), (wqkv_hi[:, c], wqkv_lo[:, c]), NN)

    if wide % 256:
        c = slice(full * 256, wide)
        qkv_ref[:, c] = dot3((n_hi[...], n_lo[...]), (wqkv_hi[:, c], wqkv_lo[:, c]), NN)

    att_ref[...] = jnp.zeros_like(att_ref)
    dqkv_ref[...] = jnp.zeros_like(dqkv_ref)
    is_last = flag_ref[0] > 0
    low_q = lax.broadcasted_iota(jnp.int32, (half, half), 0) >= half // 2
    low_k = lax.broadcasted_iota(jnp.int32, (half, half), 1) >= half // 2
    blocked = jnp.logical_and(low_q != low_k, is_last)
    norm = 1.0 / math.sqrt(HEAD)

    @pl.loop(0, 2)
    def _(w):
        r = pl.ds(pl.multiple_of(w * half, 16), half)
        for h in range(heads):
            lo, hi = head_lanes(h)
            lane = lax.broadcasted_iota(jnp.int32, (half, hi - lo), 1) + lo
            mine = jnp.logical_and(lane >= h * HEAD, lane < (h + 1) * HEAD)

            def part(i):
                return qkv_ref[r, i * inner + lo:i * inner + hi]

            q = split(jnp.where(mine, part(0) * norm, 0.0))
            k = split(part(1))
            v = split(part(2))
            do = split(jnp.where(mine, datt_ref[r, lo:hi], 0.0))
            s = dot3(q, k, NT)
            s = jnp.where(blocked, -1e30, s)
            e = jnp.exp(s - jnp.max(s, axis=-1, keepdims=True))
            p32 = e / jnp.sum(e, axis=-1, keepdims=True)
            p = split(p32)
            o = dot3(p, v, NN)
            att_ref[r, lo:hi] += jnp.where(mine, o, 0.0)
            dp = dot3(do, v, NT)
            delta = jnp.sum(dp * p32, axis=-1, keepdims=True)
            ds = split(p32 * (dp - delta))
            dv = dot3(p, do, TN)
            dq = jnp.where(mine, dot3(ds, k, NN) * norm, 0.0)
            dk = dot3(ds, q, TN)
            dqkv_ref[r, lo:hi] += dq
            dqkv_ref[r, inner + lo:inner + hi] += dk
            dqkv_ref[r, 2 * inner + lo:2 * inner + hi] += dv

    a = split(att_ref[...])
    a_hi[...], a_lo[...] = a

    @pl.loop(0, width // 256)
    def _(j):
        c = pl.ds(pl.multiple_of(j * 256, 256), 256)
        out_ref[:, c] = t_ref[:, c] + dot3(a, (wo_hi[:, c], wo_lo[:, c]), NN)

    d_hi[...], d_lo[...] = split(dqkv_ref[...])

    @pl.loop(0, width // 256)
    def _(j):
        c = pl.ds(pl.multiple_of(j * 256, 256), 256)
        dt_ref[:, c] = dot3((d_hi[...], d_lo[...]), (wqkv_hi[c, :], wqkv_lo[c, :]), NT)

    dgain_ref[...] = jnp.zeros_like(dgain_ref)

    @pl.loop(0, rows // step)
    def _(i):
        r = pl.ds(pl.multiple_of(i * step, step), step)
        dn = dt_ref[r, :]
        xhat = xhat_ref[r, :]
        dgain_ref[...] += jnp.sum(dn * xhat, axis=0, keepdims=True)
        dx = dn * gain_ref[...]
        m1 = jnp.mean(dx, axis=-1, keepdims=True)
        m2 = jnp.mean(dx * xhat, axis=-1, keepdims=True)
        dt_ref[r, :] = g_ref[r, :] + rstd_ref[r, :] * (dx - m1 - xhat * m2)


def compute(flag, t, g, gain, wq, wk, wv, wo):
    rows, width = t.shape
    inner = wo.shape[0]
    vm = pl.BlockSpec(memory_space=pltpu.VMEM)
    anyspace = pl.BlockSpec(memory_space=pl.ANY)
    f = jax.ShapeDtypeStruct
    return pl.pallas_call(
        compute_kernel,
        out_shape=(
            f((rows, width), F32), f((rows, width), F32), f((1, width), F32),
            f((rows, width), BF16), f((rows, width), BF16), f((rows, width), BF16), f((rows, width), BF16),
            f((rows, inner), BF16), f((rows, inner), BF16),
            f((rows, 3 * inner), BF16), f((rows, 3 * inner), BF16),
        ),
        in_specs=[pl.BlockSpec(memory_space=pltpu.SMEM), vm, vm, vm] + [anyspace] * 4,
        out_specs=[vm] * 11,
        scratch_shapes=[
            pltpu.VMEM((2, width, inner), F32), pltpu.VMEM((inner, width), F32),
            pltpu.VMEM((width, 3 * inner), BF16), pltpu.VMEM((width, 3 * inner), BF16),
            pltpu.VMEM((inner, width), BF16), pltpu.VMEM((inner, width), BF16),
            pltpu.VMEM((rows, width), F32), pltpu.VMEM((rows, 1), F32),
            pltpu.VMEM((rows, 3 * inner), F32), pltpu.VMEM((rows, inner), F32),
            pltpu.VMEM((rows, inner), F32), pltpu.VMEM((rows, 3 * inner), F32),
            pltpu.SemaphoreType.DMA((4,)),
        ],
        compiler_params=pltpu.CompilerParams(vmem_limit_bytes=60 * 2**20),
        name="window_block",
    )(flag, t, g, gain, wq, wk, wv, wo)


MESH = pl.DeviceIdType.MESH
SLOTS = 256
TROWS = 304
SHARD = 40


def tile_rows_map():
    def block(r0, c0, cols):
        return [(r0 + i) * 24 + c0 + j for i in range(6) for j in range(cols)]

    none = [-5] * 4
    order = block(6, 6, 12) + block(6, 18, 6) + none + block(0, 6, 12) + block(0, 18, 6) + none
    order += none + block(6, 0, 6) + none + block(0, 0, 6)
    return np.array(order, np.int32)


def split3(x):
    hi = x.astype(BF16)
    rest = x - hi.astype(F32)
    mid = rest.astype(BF16)
    return hi, mid, (rest - mid.astype(F32)).astype(BF16)


def pick(onehot, x, dims):
    hi, mid, lo = split3(x)
    return (dot(onehot, hi, dims) + dot(onehot, mid, dims)) + dot(onehot, lo, dims)


def onehot(cond):
    return jnp.where(cond, 1.0, 0.0).astype(BF16)


def swap_matrix():
    j = lax.broadcasted_iota(jnp.int32, (SLOTS, SLOTS), 0)
    i = lax.broadcasted_iota(jnp.int32, (SLOTS, SLOTS), 1)
    b = jnp.right_shift(j, 4)
    a = jnp.bitwise_and(jnp.right_shift(j, 1), 7)
    return onehot(i == a * 32 + b * 2 + jnp.bitwise_and(j, 1))


def flip_low(i):
    return i + 1 - 2 * (i % 2)


def flip_far(i):
    return 3 - i


def remote(src, dst, send, recv, device):
    copy = pltpu.make_async_remote_copy(
        src_ref=src, dst_ref=dst, send_sem=send, recv_sem=recv, device_id=device, device_id_type=MESH
    )
    copy.start()
    return copy


def enter(a, b, diagonal):
    barrier = pltpu.get_barrier_semaphore()
    peers = [(a, (b + k) % 16) for k in range(1, 16)] + [((a + k) % 8, b) for k in range(1, 8)]
    if diagonal:
        peers += [((a + 1) % 8, (b + 1) % 16), ((a + 7) % 8, (b + 15) % 16)]
    for peer in peers:
        pl.semaphore_signal(barrier, inc=1, device_id=peer, device_id_type=MESH)
    pl.semaphore_wait(barrier, len(peers))


def rows_at(start, size):
    return pl.ds(pl.multiple_of(start, size), size)


def send_lon(src, dst, send, recv, a, b):
    copies = []
    for k in range(1, 16):
        peer = (b + k) % 16
        copies.append(remote(
            src.at[rows_at(peer * 16, 16)], dst.at[rows_at(b * 16, 16)], send.at[k - 1], recv.at[k - 1], (a, peer)
        ))
    dst[rows_at(b * 16, 16), :] = src[rows_at(b * 16, 16), :]
    return copies


def send_lat(src, dst, send, recv, a, b):
    copies = []
    for k in range(1, 8):
        peer = (a + k) % 8
        copies.append(remote(
            src.at[rows_at(peer * 32, 32)], dst.at[rows_at(a * 32, 32)], send.at[k - 1], recv.at[k - 1], (peer, b)
        ))
    dst[rows_at(a * 32, 32), :] = src[rows_at(a * 32, 32), :]
    return copies


def finish(copies):
    for copy in copies:
        copy.wait()


def front_kernel(
    cell_ref, row_ref, slot_ref, enc_ref, mask_ref, cot_ref,
    t_ref, g_ref, seat_ref,
    tile_t, tile_g, land_t, land_g, sa0, ra0, sb0, rb0, sa1, ra1, sb1, rb1,
    halo_s, halo_r, lon_s, lon_r, lat_s, lat_r,
):
    a, b = lax.axis_index("lat"), lax.axis_index("lon")
    width = cot_ref.shape[1]
    part = width // 2
    enter(a, b, True)

    seats = lax.broadcasted_iota(jnp.int32, (SLOTS, enc_ref.shape[0]), 0)
    to2 = onehot(seats == row_ref[1:2, :])
    sa0[:, :part] = pick(to2, enc_ref[:, :part], NN)
    cells = jnp.broadcast_to(slot_ref[...] + 1, (enc_ref.shape[0], 128)).astype(F32)
    sa0[:, part:] = pick(to2, cells, NN)
    go0 = send_lon(sa0, ra0, lon_s.at[0], lon_r.at[0], a, b)
    to1 = onehot(seats == row_ref[0:1, :])
    sa1[...] = pick(to1, enc_ref[:, part:], NN)
    go1 = send_lat(sa1, ra1, lat_s.at[0], lat_r.at[0], a, b)

    down, left = (a + 7) % 8, (b + 15) % 16

    def halo(tile, land, whole, first):
        moves = (
            (224, 40, land.at[pl.ds(0, 40)], (a, left)), (112, 72, whole.at[pl.ds(72, 72)], (down, b)),
            (184, 40, land.at[pl.ds(40, 40)], (down, b)), (264, 40, land.at[pl.ds(80, 40)], (down, left)),
        )
        return [
            remote(tile.at[pl.ds(row, size)], dst, halo_s.at[first + i], halo_r.at[first + i], device)
            for i, (row, size, dst, device) in enumerate(moves)
        ]

    def settle(tile, land, whole):
        whole[0:72, :] = tile[0:72, :]
        whole[144:180, :] = tile[72:108, :]
        whole[180:216, :] = land[4:40, :]
        whole[216:252, :] = land[40:76, :]
        whole[252:288, :] = land[84:120, :]

    grid = lax.broadcasted_iota(jnp.int32, (cot_ref.shape[0], TROWS), 0)
    place = onehot(grid == cell_ref[...])
    for j in range(0, width, 256):
        tile_g[:, j:j + 256] = pick(place, cot_ref[:, j:j + 256], TN)
    halo_g = halo(tile_g, land_g, g_ref, 0)

    swap = swap_matrix()
    finish(go0)
    sb0[...] = pick(swap, ra0[...], TN)
    go0 = send_lat(sb0, rb0, lat_s.at[1], lat_r.at[1], a, b)
    finish(go1)
    sb1[...] = pick(swap, ra1[...], NN)
    go1 = send_lon(sb1, rb1, lon_s.at[1], lon_r.at[1], a, b)

    finish(halo_g)
    settle(tile_g, land_g, g_ref)

    finish(go0)
    seat_ref[...] = rb0[:, part:]
    table = onehot(rb0[:, part:part + 1] == (cell_ref[...] + 1).astype(F32))
    seen = jnp.sum(table.astype(F32), axis=0, keepdims=True)
    first = lax.broadcasted_iota(jnp.int32, (16, 1), 0) == 0
    unseen = jnp.where(first, 1.0 - seen, 0.0).astype(BF16)
    mask = jnp.broadcast_to(mask_ref[...], (16, width))
    tile_t[:, :part] = pick(table, rb0[:, :part], TN) + pick(unseen, mask[:, :part], TN)
    table2 = dot(swap, table, NN).astype(BF16)
    finish(go1)
    tile_t[:, part:] = pick(table2, rb1[...], TN) + pick(unseen, mask[:, part:], TN)
    halo_t = halo(tile_t, land_t, t_ref, 4)
    finish(halo_t)
    settle(tile_t, land_t, t_ref)


def front(cell, row, slot, enc, mask, cot):
    rows, width = cot.shape
    part = width // 2
    vm = pl.BlockSpec(memory_space=pltpu.VMEM)
    f = jax.ShapeDtypeStruct
    dma = pltpu.SemaphoreType.DMA
    v = pltpu.VMEM
    return pl.pallas_call(
        front_kernel,
        out_shape=(f((rows, width), F32), f((rows, width), F32), f((SLOTS, 128), F32)),
        in_specs=[vm] * 6,
        out_specs=[vm] * 3,
        scratch_shapes=[
            v((TROWS, width), F32), v((TROWS, width), F32), v((120, width), F32), v((120, width), F32),
        ] + [v((SLOTS, part + 128), F32)] * 4 + [v((SLOTS, part), F32)] * 4 + [
            dma((8,)), dma((8,)), dma((2, 15)), dma((2, 15)), dma((2, 7)), dma((2, 7)),
        ],
        compiler_params=pltpu.CompilerParams(
            vmem_limit_bytes=60 * 2**20, collective_id=0, has_side_effects=True
        ),
        name="front",
    )(cell, row, slot, enc, mask, cot)


def tail_kernel(
    cell_ref, seat_ref, index_ref, out_ref, dt_ref, dgain_ref,
    n_hi, n_lo, g_hi, g_lo, a_hi, a_lo, d_hi, d_lo,
    decoded_ref, grads_ref, vec_ref, enc_ref,
    tile_d, tile_o, sa, ra, sb, rb, grad, acc, r1, r2, r3, r4, r5, vr,
    halo_s, halo_r, lon_s, lon_r, lat_s, lat_r, sum_s, sum_r, vec_s, vec_r,
):
    a, b = lax.axis_index("lat"), lax.axis_index("lon")
    x, c = a // 2, a % 2
    y, z = b // 4, b % 4
    width = dt_ref.shape[1]
    inner = a_hi.shape[1]
    part = width // 2
    scale = 1.0 / 192.0

    enter(a, b, True)

    up, right = (a + 1) % 8, (b + 1) % 16

    def halo(src, tile, first):
        moves = (
            (72, 72, 112, (up, b)), (216, 40, 184, (up, b)), (176, 40, 224, (a, right)), (248, 40, 264, (up, right)),
        )
        copies = []
        for i, (row, size, to, device) in enumerate(moves):
            copies.append(remote(
                src.at[pl.ds(row, size)], tile.at[pl.ds(to, size)], halo_s.at[first + i], halo_r.at[first + i], device
            ))
        tile[0:72, :] = src[0:72, :]
        tile[72:112, :] = src[144:184, :]
        return copies

    halo_d = halo(dt_ref, tile_d, 0)
    halo_o = halo(out_ref, tile_o, 4)

    def weight_grad(m):
        if m == 0:
            left = jnp.concatenate([a_hi[...], a_hi[...], a_lo[...]], axis=0)
            for i in range(2):
                cols = slice(i * part, (i + 1) * part)
                gh, gl = g_hi[:, cols], g_lo[:, cols]
                res = dot(left, jnp.concatenate([gh, gl, gh], axis=0), TN)
                grad[m, :, :, i] = res.reshape(4, 4, SHARD, inner)
        else:
            which = 3 - m
            cols = slice(which * inner, (which + 1) * inner)
            dh, dl = d_hi[:, cols], d_lo[:, cols]
            right3 = jnp.concatenate([dh, dl, dh], axis=0)
            for i in range(2):
                half = slice(i * part, (i + 1) * part)
                nh, nl = n_hi[:, half], n_lo[:, half]
                res = dot(jnp.concatenate([nh, nh, nl], axis=0), right3, TN)
                grad[m, 2 * i:2 * i + 2] = res.reshape(2, 4, 2, SHARD, inner)

    class Sum:
        def __init__(self, m):
            self.m = m
            self.first = m % 2 == 0
            self.q1, self.q2 = (flip_low, flip_far) if m < 2 else (flip_far, flip_low)
            self.stage = 0
            self.copies = []

        def chunk(self, i):
            return acc.at[self.m, i] if self.first else acc.at[self.m, :, i]

        def piece(self, i):
            return acc.at[self.m, y, i] if self.first else acc.at[self.m, i, z]

        def device1(self, i):
            return (a, i * 4 + z) if self.first else (a, y * 4 + i)

        def device2(self, i):
            return (a, y * 4 + i) if self.first else (a, i * 4 + z)

        def send(self, k, src, dst, device):
            self.copies.append(remote(src, dst, sum_s.at[self.m, k], sum_r.at[self.m, k], device))

        def begin(self):
            m, s = self.m, self.stage
            me1, me2 = (y, z) if self.first else (z, y)
            if s == 0:
                self.send(0, grad.at[m, :, :, 1 - c], acc.at[m], (a + 1 - 2 * c, b))
            elif s == 1:
                p = self.q1(me1)
                self.send(1, self.chunk(p), r1.at[m, 0], self.device1(p))
                self.send(2, self.chunk(self.q2(p)), r1.at[m, 1], self.device1(p))
            elif s == 2:
                p = self.q2(me1)
                self.send(3, self.chunk(p), r2.at[m], self.device1(p))
            elif s == 3:
                p = self.q1(me2)
                self.send(4, self.piece(p), r3.at[m, 0], self.device2(p))
                self.send(5, self.piece(self.q2(p)), r3.at[m, 1], self.device2(p))
            elif s == 4:
                p = self.q2(me2)
                self.send(6, self.piece(p), r4.at[m], self.device2(p))
            elif s == 5:
                self.send(7, self.piece(me2), r5.at[m, 0], (flip_low(x) * 2 + c, b))
            elif s == 6:
                self.send(8, self.piece(me2), r5.at[m, 1], (flip_far(x) * 2 + c, b))
            elif s == 7:
                self.send(9, grads_ref.at[m, c], grads_ref.at[m, c], (a + 1 - 2 * c, b))

        def end(self):
            m, s = self.m, self.stage
            me1, me2 = (y, z) if self.first else (z, y)
            finish(self.copies)
            self.copies = []
            if s == 0:
                @pl.loop(0, 4)
                def _(i):
                    acc[m, i] += grad[m, i, :, c]
            elif s == 1:
                for i in range(4):
                    for k, me in enumerate((me1, self.q2(me1))):
                        if self.first:
                            acc[m, me, i] += r1[m, k, i]
                        else:
                            acc[m, i, me] += r1[m, k, i]
            elif s == 2:
                for i in range(4):
                    if self.first:
                        acc[m, me1, i] += r2[m, i]
                    else:
                        acc[m, i, me1] += r2[m, i]
            elif s == 3:
                for k, me in enumerate((me2, self.q2(me2))):
                    if self.first:
                        acc[m, y, me] += r3[m, k]
                    else:
                        acc[m, me, z] += r3[m, k]
            elif s == 4:
                acc[m, y, z] += r4[m]
            elif s == 5:
                acc[m, y, z] += r5[m, 0]
            elif s == 6:
                grads_ref[m, c] = (acc[m, y, z] + r5[m, 1]) * scale
            self.stage += 1

        def step(self):
            self.end()
            if self.stage < 8:
                self.begin()

    sums = [Sum(m) for m in range(4)]

    vec_devices = [
        (a + 1 - 2 * c, b), (flip_low(x) * 2 + c, b), (flip_far(x) * 2 + c, b),
        (a, flip_low(y) * 4 + z), (a, flip_far(y) * 4 + z), (a, y * 4 + flip_low(z)), (a, y * 4 + flip_far(z)),
    ]
    vec_copies = []

    def vec_begin(k):
        vec_copies.append(remote(vec_ref, vr.at[k], vec_s.at[k], vec_r.at[k], vec_devices[k]))

    def vec_step():
        k = len(vec_copies) - 1
        vec_copies[k].wait()
        vec_ref[...] += vr[k]
        if k < 6:
            vec_begin(k + 1)

    weight_grad(0)
    sums[0].begin()

    finish(halo_d)
    table = onehot(seat_ref[:, 0:1] == (cell_ref[...] + 1).astype(F32))
    swap = swap_matrix()
    table2 = dot(swap, table, NN).astype(BF16)
    sa[0] = pick(table, tile_d[:, :part], NN)
    back0 = send_lat(sa.at[0], ra.at[0], lat_s.at[0], lat_r.at[0], a, b)
    sa[1] = pick(table2, tile_d[:, part:], NN)
    back1 = send_lon(sa.at[1], ra.at[1], lon_s.at[1], lon_r.at[1], a, b)
    seen = jnp.sum(table.astype(F32), axis=0, keepdims=True)
    masked = jnp.where(cell_ref[...] >= 0, 1.0 - seen, 0.0)
    masked = jnp.broadcast_to(masked, (8, TROWS)).astype(BF16)
    vec_ref[...] = pick(masked, tile_d[...], NN) * scale
    vec_ref[1:2, :] = dgain_ref[...] * scale
    vec_begin(0)

    weight_grad(1)
    sums[1].begin()
    sums[0].step()
    weight_grad(2)
    sums[2].begin()
    sums[1].step()

    finish(back0)
    sb[0] = pick(swap, ra[0], NN)
    back0 = send_lon(sb.at[0], rb.at[0], lon_s.at[0], lon_r.at[0], a, b)
    finish(back1)
    sb[1] = pick(swap, ra[1], TN)
    back1 = send_lat(sb.at[1], rb.at[1], lat_s.at[1], lat_r.at[1], a, b)

    weight_grad(3)
    sums[3].begin()
    sums[2].step()
    vec_step()

    finish(halo_o)
    cells = lax.broadcasted_iota(jnp.int32, (decoded_ref.shape[0], TROWS), 0)
    place = onehot(cells == cell_ref[...])
    for j in range(0, width, 256):
        decoded_ref[:, j:j + 256] = pick(place, tile_o[:, j:j + 256], NN)

    sums[3].step()
    sums[0].step()
    vec_step()

    finish(back0)
    finish(back1)
    slots = lax.broadcasted_iota(jnp.int32, (enc_ref.shape[0], SLOTS), 1)
    enc_ref[:, :part] = pick(onehot(slots == index_ref[:, 1:2]), rb[0], NN)
    enc_ref[:, part:] = pick(onehot(slots == index_ref[:, 0:1]), rb[1], NN)

    while any(total.stage < 8 for total in sums):
        front = min(total.stage for total in sums)
        for total in sums:
            if total.stage == front:
                total.step()
        if len(vec_copies) < 7:
            vec_step()
    vec_step()


def tail(cell, slot, index, out, dt, dgain, acts):
    rows, width = dt.shape
    inner = acts[4].shape[1]
    part = width // 2
    vm = pl.BlockSpec(memory_space=pltpu.VMEM)
    f = jax.ShapeDtypeStruct
    dma = pltpu.SemaphoreType.DMA
    v = pltpu.VMEM
    return pl.pallas_call(
        tail_kernel,
        out_shape=(
            f((rows, width), F32), f((4, 2, SHARD, inner), F32), f((8, width), F32), f((index.shape[0], width), F32),
        ),
        in_specs=[vm] * 14,
        out_specs=[vm] * 4,
        scratch_shapes=[
            v((TROWS, width), F32), v((TROWS, width), F32),
            v((2, SLOTS, part), F32), v((2, SLOTS, part), F32), v((2, SLOTS, part), F32), v((2, SLOTS, part), F32),
            v((4, 4, 4, 2, SHARD, inner), F32), v((4, 4, 4, SHARD, inner), F32),
            v((4, 2, 4, SHARD, inner), F32), v((4, 4, SHARD, inner), F32),
            v((4, 2, SHARD, inner), F32), v((4, SHARD, inner), F32), v((4, 2, SHARD, inner), F32),
            v((7, 8, width), F32),
            dma((8,)), dma((8,)), dma((2, 15)), dma((2, 15)), dma((2, 7)), dma((2, 7)),
            dma((4, 10)), dma((4, 10)), dma((7,)), dma((7,)),
        ],
        compiler_params=pltpu.CompilerParams(
            vmem_limit_bytes=60 * 2**20, collective_id=1, has_side_effects=True
        ),
        name="tail",
    )(cell, slot, index, out, dt, dgain, *acts)


def body(positions, encoded, mask_token, norm_gain, w_query, w_key, w_value, w_out, cotangent):
    tile_rows, tile_cols, model_width = cotangent.shape
    lat_count = lax.axis_size("lat")
    lon_count = lax.axis_size("lon")
    devices = lat_count * lon_count
    grid_lat = lat_count * tile_rows
    grid_lon = lon_count * tile_cols
    tile_size = tile_rows * tile_cols
    capacity = tile_size // devices
    lat_cell = positions // grid_lon
    lon_cell = positions % grid_lon
    target = lat_cell // tile_rows * lon_count + lon_cell // tile_cols
    cell_slot = lat_cell % tile_rows * tile_cols + lon_cell % tile_cols
    serial = jnp.arange(positions.shape[0])
    earlier = jnp.logical_and(target[None, :] == target[:, None], serial[None, :] < serial[:, None])
    rank = jnp.sum(earlier.astype(jnp.int32), axis=1)
    buffer_index = target * capacity + rank
    index2 = (target % lon_count) * (lat_count * capacity) + (target // lon_count) * capacity + rank
    row = jnp.stack([buffer_index, index2], axis=0)
    tile_map = jnp.asarray(tile_rows_map())[None]
    tokens, grad_rolled, seat = front(
        tile_map, row, cell_slot[:, None], encoded, mask_token[None], cotangent.reshape(tile_size, model_width)
    )
    is_last = lax.axis_index("lat") == lat_count - 1
    flag = is_last.astype(jnp.int32).reshape(1)
    out_rolled, grad_tile, grad_gain, *acts = compute(
        flag, tokens, grad_rolled, norm_gain[None], w_query, w_key, w_value, w_out
    )
    decoded, grads, vec, grad_encoded = tail(tile_map, seat, row.T, out_rolled, grad_tile, grad_gain, acts)
    decoded = decoded.reshape(tile_rows, tile_cols, model_width)
    b = lax.axis_index("lon")
    share = model_width // lon_count
    own = lax.dynamic_slice(vec, (0, b * share), (2, share))
    rows = grads.reshape(4, share, -1)
    grad_out = jnp.concatenate([grads[0, 0], grads[0, 1]], axis=1)
    return (decoded, rows[3], rows[2], rows[1], grad_out, own[0], own[1], grad_encoded)


def solution(mesh):
    return jax.shard_map(
        body,
        mesh=mesh,
        in_specs=(
            P(("lat", "lon")),
            P(("lat", "lon"), None),
            P(),
            P(),
            P(),
            P(),
            P(),
            P(),
            P("lat", "lon", None),
        ),
        out_specs=(
            P("lat", "lon", None),
            P("lon", None),
            P("lon", None),
            P("lon", None),
            P("lon", None),
            P("lon"),
            P("lon"),
            P(("lat", "lon"), None),
        ),
        check_vma=False,
    )
```

time: 445 us -> 218 us (0.49); the launches traced: 437 us -> 217 us
  Pallas kernels: 0 us -> 204 us
  local copies, waits for them, and re-layouts: 126 us -> 9.6 us
  matrix products: 102 us -> 0 us
  blocking collectives: 80.6 us -> 0 us
  waiting for transfers between devices: 39.4 us -> 0 us
  other arithmetic: 39 us -> 2.83 us
  starting transfers between devices: 35.7 us -> 0 us
  between operations: 14.8 us -> 0.72 us
    pallas_call x0 -> x3, Pallas kernels: none -> 204 us  [the longest x1 112 us: tail(): pl.pallas_call(tail_kernel, out_shape=(f((rows, width), F32), f((4, 2, SH...]
    dot_general x18 -> x0, matrix products: 102 us -> none  [the longest x3 20.1 us: window_block(): jnp.dot(attended, out_w, precision=highest)]
    psum x1 -> x0, blocking collectives: 80.6 us -> none  [body(): lax.psum((grad_query * scale, grad_key * scale, grad_value * scale, grad_...]
    reshape x15 -> x0, local copies, waits for them, and re-layouts: 37.6 us -> none  [the longest x2 5.35 us: window_block(): tile_grid.reshape(tile_rows, window_count, tile_rows, model_width)]
    all_to_all x3 -> x0, starting transfers between devices: 27.2 us -> none  [the longest x1 11.1 us: body(): lax.all_to_all(send_slot.reshape(devices, capacity), ('lat', 'lon'), spli...]
    ppermute x8 -> x0, waiting for transfers between devices: 25 us -> none  [passed_along(): return lax.ppermute(block, axis, route)]
    transpose x9 -> x0, local copies, waits for them, and re-layouts: 23.1 us -> none  [the longest x2 6.8 us: window_block(): tile_grid.reshape(tile_rows, window_count, tile_rows, model_width)]
    concatenate x7 -> x1, other arithmetic: 17 us -> 0.69 us  [body(): grad_out = jnp.concatenate([grads[0, 0], grads[0, 1]], axis=1)]
  transfers between devices with their start and end apart: 12 -> 0, of which waited for: 4 -> 0; matrix products, arithmetic and copies ran while one was open for 33% -> 0% of each run, Pallas kernels for 0% -> 0%
where the time goes in v1:
time: 218 us; the launch traced here: 217 us
  Pallas kernels  204 us (94%)
  local copies, waits for them, and re-layouts  9.6 us (4%)
  other arithmetic  2.83 us (1%)
    pallas_call x1, Pallas kernels, tail(): pl.pallas_call(tail_kernel, out_shape=(f((rows, width), F32), f((4, 2, SH...  112 us
    pallas_call x1, Pallas kernels, front(): pl.pallas_call(front_kernel, out_shape=(f((rows, width), F32), f((rows, w...  49.7 us
    pallas_call x1, Pallas kernels, compute(): pl.pallas_call(compute_kernel, out_shape=(f((rows, width), F32), f((rows,...  41.5 us

profile of v1, /device:TPU:0, one launch (start us, length us, event | category | flops | bytes accessed | tf_op | source)
XLA Modules:
  0.0 216.7 jit_solution(12028439203450611121)
XLA Ops:
  0.6 0.0 copy-start.3
  0.6 0.7 fusion.8
  1.3 0.7 fusion.6
  2.0 0.2 convert_reduce_fusion
  2.2 0.6 pad_add_fusion.row_ref
  2.8 0.7 copy.24.slot_ref
  3.5 1.3 broadcast_in_dim.18.mask_ref
  4.8 49.7 %front.1 = (f32[288,1280]{1,0:T(8,128)}, f32[288,1280]{1,0:T(8,128)}, f32[256,128]{1,0:T(8,128)}) custom-call(s32[1,304]{1,0:T(1,128)} %constant.90.cell_ref, s32[2,72]{1,0:T(2,128)} %pad_add_fusion.row_ref, s32[72,1]{1,0:T(8,128)} %copy.24.slot_ref, f32[72,1280]{1,0:T(8,128)} %enc_ref.1, f32[1,1280]{1,0:T(1,128)} %broadcast_in_dim.18.mask_ref, ...), custom_call_target="tpu_custom_call" | custom-call | tf_op jit(solution)/shard_map/front/pallas_call | solution.py:384
  54.5 0.0 copy-done.3
  54.5 0.6 broadcast_in_dim.19.gain_ref
  55.1 0.0 copy-start.2
  55.1 41.5 %window_block.1 = (f32[288,1280]{1,0:T(8,128)}, f32[288,1280]{1,0:T(8,128)}, f32[1,1280]{1,0:T(1,128)}, bf16[288,1280]{1,0:T(8,128)(2,1)}, bf16[288,1280]{1,0:T(...) custom-call(s32[1]{0:T(128)} %bitcast.5.flag_ref, ...), custom_call_target="tpu_custom_call" | custom-call | tf_op jit(solution)/shard_map/window_block/pallas_call | solution.py:183
  96.6 0.0 copy-done.2
  96.6 0.7 copy.25
  97.4 112.4 %tail.1 = (f32[288,1280]{1,0:T(8,128)}, f32[4,2,40,640]{3,2,1,0:T(8,128)}, f32[8,1280]{1,0:T(8,128)}, f32[72,1280]{1,0:T(8,128)}) custom-call(s32[1,304]{1,0:T(1,128)} %constant.90.cell_ref, f32[256,128]{1,0:T(8,128)} %get-tuple-element.26.seat_ref, s32[72,2]{1,0:T(8,128)} %bitcast.26, f32[288,1280]{1,0:T(8,128)} %get-tuple-element.29.out_ref, ...), custom_call_target="tpu_custom_call" | custom-call | tf_op jit(solution)/shard_map/tail/pallas_call | solution.py:634
  209.7 0.0 copy-start
  209.7 1.1 slice_bitcast_fusion.1
  210.8 0.7 pad_maximum_fusion
  211.5 2.0 fusion.9
  213.5 0.8 constant_dynamic-slice_fusion
  214.2 0.5 slice_bitcast_fusion.2
  214.8 0.0 copy-done
  214.8 0.0 copy-start.1
  214.8 1.1 copy.28
  215.9 0.1 copy-done.1
  216.0 0.7 copy.29
  (1 shorter events, 0.0 us)
Async XLA Ops:
  0.6 53.9 %copy-start.3 = (f32[1280]{0:T(1024)S(1)}, f32[1280]{0:T(1024)}, u32[]{:S(2)}) copy-start(f32[1280]{0:T(1024)} %param.13) | copy-start | bytes 15364
  55.1 41.5 %copy-start.2 = (s32[2,72]{1,0:T(2,128)S(1)}, s32[2,72]{1,0:T(2,128)}, u32[]{:S(2)}) copy-start(s32[2,72]{1,0:T(2,128)} %pad_add_fusion.row_ref) | copy-start | bytes 1732
  209.7 5.0 %copy-start = (f32[288,1280]{1,0:T(8,128)S(1)}, f32[288,1280]{1,0:T(8,128)}, u32[]{:S(2)}) copy-start(f32[288,1280]{1,0:T(8,128)} %get-tuple-element.40) | copy-start | bytes 4423684
  214.8 1.2 copy-start.1
